TPU v7x, 32 devices: a whole 2x2x4 slice. The times are simulated.
32 devices in a mesh: row: 8 (over y, x, core), col: 4 (over z).
Axes of the slice: x: 2, y: 2, z: 4, core: 2. Of those that a mesh axis runs over, the one named last changes fastest.
Arguments:
- tokens: bfloat16 [32768, 768], P(('row', 'col')), may hold values from -6 to 6
- gate_prob: bfloat16 [32768], P(('row', 'col')), may hold values from 0.19921875 to 1
- expert_id: int32 [32768], P(('row', 'col')), may hold values from 0 to 63, as said below
- dest_row: int32 [32768], P(('row', 'col')), may hold values from 0 to 32767, as said below
- ff_gain: float32 [768], replicated, may hold values from 0.5 to 1.5
- expert_in: bfloat16 [64, 768, 3072], P(('row', 'col')), may hold values from -0.21875 to 0.21875
- expert_out: bfloat16 [64, 3072, 768], P(('row', 'col')), may hold values from -0.109375 to 0.109375
- attn_gain: float32 [768], replicated, may hold values from 0.5 to 1.5
- qkv_weight: bfloat16 [768, 2304], P(None, 'row'), may hold values from -8 to 8
- mix_weight: bfloat16 [768, 768], P(None, 'row'), may hold values from -1.75 to 1.75
Outputs:
- moe_out: bfloat16 [32768, 768], P(('row', 'col'))
- attn_branch: bfloat16 [32768, 768], P(('row', 'col'))
Inputs may be any that keep to these rules, and one draw needn't show every extreme that they name: `expert_id`: expert e's weights are held by device e // 2 (its local index e % 2). Each expert is named by at most 768 tokens in all, and some expert by exactly 768. Within the rows of one device no expert is named more than 26 times, and some device names some expert exactly 26 times. The rows of one device name the experts of any one device, together, exactly 32 times. `dest_row`: A permutation of all rows. Owner device o holds rows o * 1024 to (o + 1) * 1024 - 1; the rows of every device go to every owner exactly 32 times, and of the rows whose experts one device holds, exactly 32 go to every owner.
All inputs are finite; a program needn't handle non-finite values.
Results may differ from a plain program's by a relative error of at most 0.012.
Values may be sent and summed in bfloat16 or wider, within the bound.
A program may use at most 128 MiB of HBM per device.

v0:
```python
import functools

import jax
import jax.numpy as jnp
from jax import lax
from jax.experimental import pallas as pl
from jax.experimental.pallas import tpu as pltpu
from jax.sharding import PartitionSpec as P

HEAD_DIM = 64
SEQ = 512
LANES = 128
DIGIT = 32
EPSILON = 1e-06
BF16 = jnp.bfloat16
F32 = jnp.float32
I32 = jnp.int32
NT = (((1,), (1,)), ((), ()))
MIB = 1 << 20


def iota(shape, axis):
    return lax.broadcasted_iota(I32, shape, axis)


def dot(a, b):
    return jnp.dot(a, b, preferred_element_type=F32)


def dot_nt(a, b):
    return lax.dot_general(a, b, NT, preferred_element_type=F32)


def one(mask):
    return jnp.where(mask, 1.0, 0.0).astype(BF16)


def rms_scale(values, gain):
    widened = values.astype(F32)
    power = jnp.mean(widened * widened, axis=-1, keepdims=True)
    return (widened * lax.rsqrt(power + EPSILON) * gain).astype(BF16)


def earlier(rows):
    return one(iota((rows, rows), 0) < iota((rows, rows), 1))


def permute(place, rows, source, low=0, count=None):
    count = rows if count is None else count
    return dot(one(iota((count, rows), 0) + low == place), source)


def to_blocks(onehot, rank, fields, per):
    rows = rank.shape[1]
    lane = iota((LANES, rows), 0)
    value = jnp.zeros((LANES, rows), F32)
    for k, field in enumerate(fields):
        value = jnp.where(lane == rank + k * per, field, value)
    return dot_nt(onehot, value.astype(BF16))


def spread(blocks, rows, per):
    devices = blocks.shape[0]
    owner = one(iota((rows, devices), 0) // per == iota((rows, devices), 1))
    lanes = dot(owner, blocks.astype(BF16))
    keep = iota((rows, LANES), 1) % per == iota((rows, LANES), 0) % per
    return jnp.where(keep, lanes, 0.0).astype(BF16)


def field_rows(spreaded, per):
    pick = one(iota((8, LANES), 1) // per == iota((8, LANES), 0))
    return dot_nt(pick, spreaded)


def dispatch_kernel(devices, id_ref, dest_ref, gate_ref, tok_ref, out_ref, meta_ref):
    rows = tok_ref.shape[0]
    per = rows // devices
    ids = id_ref[...]
    dest = dest_ref[...]
    target = ids // 2
    local = ids - target * 2
    owner = dest // rows
    place = dest - owner * rows
    onehot = one(iota((devices, rows), 0) == target)
    counts = dot(onehot, earlier(rows))
    rank = jnp.sum(onehot.astype(F32) * counts, axis=0, keepdims=True).astype(I32)
    fields = [
        (local * DIGIT + place % DIGIT).astype(F32),
        (place // DIGIT).astype(F32),
        owner.astype(F32),
        gate_ref[...].astype(F32),
    ]
    meta_ref[...] = to_blocks(onehot, rank, fields, per)
    position = target * per + rank
    step = rows // 4
    for i in range(4):
        part = permute(position, rows, tok_ref[...], i * step, step)
        out_ref[i * step : (i + 1) * step, :] = part.astype(BF16)


def expert_kernel(
    devices, x_ref, meta_ref, gain_ref, in_ref, out_ref, y_ref, meta2_ref, xs, inputs, total, info, places
):
    rows, width = x_ref.shape
    per = rows // devices
    cap = inputs.shape[1]
    expert, chunk = pl.program_id(0), pl.program_id(1)

    @pl.when((expert == 0) & (chunk == 0))
    def _():
        spreaded = spread(meta_ref[...], rows, per)
        fields = field_rows(spreaded, per)
        code = fields[0:1].astype(I32)
        high = fields[1:2].astype(I32)
        owner = fields[2:3].astype(I32)
        local = code // DIGIT
        low = code - local * DIGIT
        onehot = one(iota((devices, rows), 0) == owner)
        first = one(jnp.broadcast_to(local == 0, (8, rows)))
        upper = earlier(rows)
        counts = dot(onehot, upper)
        rank2 = jnp.sum(onehot.astype(F32) * counts, axis=0, keepdims=True).astype(I32)
        meta2_ref[...] = to_blocks(onehot, rank2, [low.astype(F32), high.astype(F32)], per)
        leave = owner * per + rank2
        before = dot(first, upper)[0:1].astype(I32)
        number = jnp.sum(jnp.where(local == 0, 1.0, 0.0), axis=1, keepdims=True).astype(I32)
        position = jnp.where(local == 0, before, number + iota((1, rows), 1) - before)
        sort = one(iota((rows, rows), 0) == position)
        digit = iota((8, rows), 0)
        leave_digits = jnp.where(digit == 0, leave // DIGIT, leave % DIGIT).astype(F32)
        places[...] = dot_nt(leave_digits.astype(BF16), sort)
        put = one(iota((LANES, LANES), 0) // per == iota((LANES, LANES), 1))
        columns = dot(spreaded, put).astype(BF16)
        info[...] = dot(sort, columns)
        step = rows // 4
        for i in range(4):
            part = slice(i * step, (i + 1) * step)
            sorted_rows = dot(sort[part], x_ref[...]).astype(BF16)
            xs[part] = sorted_rows
            normed = rms_scale(sorted_rows, gain_ref[...])
            is_first = iota((step, 1), 0) + i * step < number
            none = jnp.zeros_like(normed)
            if (i + 1) * step <= cap:
                inputs[0, i * step : (i + 1) * step] = jnp.where(is_first, normed, none)
            if i * step >= rows - cap:
                low_row = i * step - (rows - cap)
                inputs[1, low_row : low_row + step] = jnp.where(is_first, none, normed)
        total[...] = jnp.zeros_like(total)

    base = pl.multiple_of(expert * (rows - cap), rows - cap)
    hidden = jnp.maximum(dot(inputs[expert], in_ref[0]), 0.0).astype(BF16)
    total[pl.ds(base, cap), :] += dot(hidden, out_ref[0])

    @pl.when((expert == 1) & (chunk == pl.num_programs(1) - 1))
    def _():
        gate = info[:, 3:4]
        result = total[...].astype(BF16).astype(F32)
        xs[...] = (xs[...].astype(F32) + gate * result).astype(BF16)
        leave = (places[0:1] * DIGIT + places[1:2]).astype(I32)
        step = rows // 4
        for i in range(4):
            part = permute(leave, rows, xs[...], i * step, step)
            y_ref[i * step : (i + 1) * step, :] = part.astype(BF16)


def attention_kernel(devices, x_ref, meta_ref, gain_ref, qkv_ref, mix_ref, moe_ref, branch_ref, qkv, context):
    rows, width = x_ref.shape
    per = rows // devices
    seq = moe_ref.shape[0]
    fields = field_rows(spread(meta_ref[...], rows, per), per)
    place = (fields[1:2] * DIGIT + fields[0:1]).astype(I32)
    moved = permute(place, rows, x_ref[...], pl.program_id(0) * seq, seq).astype(BF16)
    moe_ref[...] = moved
    normed = rms_scale(moved, gain_ref[...])
    for i in range(3):
        part = slice(i * width, (i + 1) * width)
        qkv[:, part] = dot(normed, qkv_ref[:, part]).astype(BF16)
    scale = 1.0 / HEAD_DIM**0.5
    left = iota((seq, LANES), 1) < HEAD_DIM
    ones = jnp.ones((seq, LANES), BF16)
    for pair in range(width // LANES):
        at = pair * LANES
        queries = qkv[:, at : at + LANES] * jnp.asarray(scale, BF16)
        keys = qkv[:, width + at : width + at + LANES]
        values = jnp.concatenate([qkv[:, 2 * width + at : 2 * width + at + LANES], ones], axis=1)
        halves = []
        for mask in (left, jnp.logical_not(left)):
            scores = dot_nt(jnp.where(mask, queries, jnp.zeros_like(queries)), keys)
            peak = jnp.max(scores, axis=1, keepdims=True)
            weights = jnp.exp(scores - peak).astype(BF16)
            mixed = dot(weights, values)
            halves.append(mixed[:, :LANES] / mixed[:, LANES:])
        context[:, at : at + LANES] = jnp.where(left, halves[0], halves[1]).astype(BF16)
    branch_ref[...] = dot(context[...], mix_ref[...]).astype(BF16)


def exchange_kernel(sizes, x_ref, m_ref, y_ref, n_ref, send, recv, send_meta, recv_meta, own):
    n_row, n_col = sizes
    devices = n_row * n_col
    per = x_ref.shape[0] // devices
    me = lax.axis_index("row") * n_col + lax.axis_index("col")

    def peer_of(i):
        return lax.rem(me + i, devices)

    def coords(device):
        return (device // n_col, lax.rem(device, n_col))

    def block(ref, device):
        return ref.at[pl.ds(pl.multiple_of(device * per, per), per)]

    barrier = pltpu.get_barrier_semaphore()

    def greet(i, carry):
        pl.semaphore_signal(
            barrier, inc=1, device_id=coords(peer_of(i)), device_id_type=pl.DeviceIdType.MESH
        )
        return carry

    lax.fori_loop(1, devices, greet, 0)
    mine = [
        pltpu.make_async_copy(block(x_ref, me), block(y_ref, me), own.at[0]),
        pltpu.make_async_copy(m_ref.at[me], n_ref.at[me], own.at[1]),
    ]
    for copy in mine:
        copy.start()
    pl.semaphore_wait(barrier, devices - 1)

    def copies(i, target, landing):
        peer = peer_of(i)
        return (
            pltpu.make_async_remote_copy(
                src_ref=m_ref.at[peer],
                dst_ref=n_ref.at[landing],
                send_sem=send_meta.at[i],
                recv_sem=recv_meta.at[i],
                device_id=coords(target),
                device_id_type=pl.DeviceIdType.MESH,
            ),
            pltpu.make_async_remote_copy(
                src_ref=block(x_ref, peer),
                dst_ref=block(y_ref, landing),
                send_sem=send.at[i],
                recv_sem=recv.at[i],
                device_id=coords(target),
                device_id_type=pl.DeviceIdType.MESH,
            ),
        )

    def begin(i, carry):
        for copy in copies(i, peer_of(i), me):
            copy.start()
        return carry

    lax.fori_loop(1, devices, begin, 0)

    def finish(i, carry):
        source = lax.rem(me + devices - i, devices)
        for copy in copies(i, peer_of(i), source):
            copy.wait_send()
            copy.wait_recv()
        return carry

    lax.fori_loop(1, devices, finish, 0)
    for copy in mine:
        copy.wait()


def exchange(x, meta, sizes, collective_id):
    devices = sizes[0] * sizes[1]
    rows, width = x.shape
    per = rows // devices
    meta = meta.reshape(devices, 1, LANES)
    if per % 16:
        y = lax.all_to_all(
            x.reshape(devices, per, width), ("row", "col"), split_axis=0, concat_axis=0, tiled=True
        )
        n = lax.all_to_all(meta, ("row", "col"), split_axis=0, concat_axis=0, tiled=True)
        return y.reshape(rows, width), n.reshape(devices, LANES)
    anywhere = pl.BlockSpec(memory_space=pl.ANY)
    y, n = pl.pallas_call(
        functools.partial(exchange_kernel, sizes),
        out_shape=(
            jax.ShapeDtypeStruct(x.shape, x.dtype),
            jax.ShapeDtypeStruct(meta.shape, meta.dtype),
        ),
        in_specs=[anywhere] * 2,
        out_specs=(anywhere, anywhere),
        scratch_shapes=[pltpu.SemaphoreType.DMA((devices,))] * 4 + [pltpu.SemaphoreType.DMA((2,))],
        compiler_params=pltpu.CompilerParams(collective_id=collective_id, has_side_effects=True),
        name="exchange%d" % collective_id,
    )(x, meta)
    return y, n.reshape(devices, LANES)


def whole(shape):
    return pl.BlockSpec(shape, lambda *_: (0,) * len(shape))


def shards(
    sizes,
    tokens,
    gate_prob,
    expert_id,
    dest_row,
    ff_gain,
    expert_in,
    expert_out,
    attn_gain,
    qkv_weight,
    mix_weight,
):
    rows, width = tokens.shape
    devices = sizes[0] * sizes[1]
    hidden = expert_in.shape[2]
    cap = rows * 3 // 4
    qkv_full = lax.all_gather(qkv_weight, "row", axis=1, tiled=True)
    mix_full = lax.all_gather(mix_weight, "row", axis=1, tiled=True)
    meta_shape = jax.ShapeDtypeStruct((devices, LANES), F32)
    rows_shape = jax.ShapeDtypeStruct((rows, width), BF16)

    leaving, meta = pl.pallas_call(
        functools.partial(dispatch_kernel, devices),
        out_shape=(rows_shape, meta_shape),
        compiler_params=pltpu.CompilerParams(vmem_limit_bytes=32 * MIB),
        name="dispatch",
    )(
        expert_id.reshape(1, rows),
        dest_row.reshape(1, rows),
        gate_prob.reshape(1, rows),
        tokens,
    )
    arrived, meta = exchange(leaving, meta, sizes, 1)

    chunk = hidden // 4
    leaving, meta = pl.pallas_call(
        functools.partial(expert_kernel, devices),
        out_shape=(rows_shape, meta_shape),
        grid=(2, hidden // chunk),
        in_specs=[
            whole((rows, width)),
            whole((devices, LANES)),
            whole((1, width)),
            pl.BlockSpec((1, width, chunk), lambda e, c: (e, 0, c)),
            pl.BlockSpec((1, chunk, width), lambda e, c: (e, c, 0)),
        ],
        out_specs=(whole((rows, width)), whole((devices, LANES))),
        scratch_shapes=[
            pltpu.VMEM((rows, width), BF16),
            pltpu.VMEM((2, cap, width), BF16),
            pltpu.VMEM((rows, width), F32),
            pltpu.VMEM((rows, LANES), F32),
            pltpu.VMEM((8, rows), F32),
        ],
        compiler_params=pltpu.CompilerParams(vmem_limit_bytes=48 * MIB),
        name="experts",
    )(arrived, meta, ff_gain.reshape(1, width), expert_in, expert_out)
    arrived, meta = exchange(leaving, meta, sizes, 2)

    return pl.pallas_call(
        functools.partial(attention_kernel, devices),
        out_shape=(rows_shape, rows_shape),
        grid=(rows // SEQ,),
        in_specs=[
            whole((rows, width)),
            whole((devices, LANES)),
            whole((1, width)),
            whole((width, 3 * width)),
            whole((width, width)),
        ],
        out_specs=(
            pl.BlockSpec((SEQ, width), lambda s: (s, 0)),
            pl.BlockSpec((SEQ, width), lambda s: (s, 0)),
        ),
        scratch_shapes=[
            pltpu.VMEM((SEQ, 3 * width), BF16),
            pltpu.VMEM((SEQ, width), BF16),
        ],
        compiler_params=pltpu.CompilerParams(vmem_limit_bytes=48 * MIB),
        name="attention",
    )(arrived, meta, attn_gain.reshape(1, width), qkv_full, mix_full)


def solution(mesh):
    placed = (
        P(("row", "col"), None),
        P(("row", "col")),
        P(("row", "col")),
        P(("row", "col")),
        P(),
        P(("row", "col"), None, None),
        P(("row", "col"), None, None),
        P(),
        P(None, "row"),
        P(None, "row"),
    )
    sizes = (mesh.shape["row"], mesh.shape["col"])
    return jax.shard_map(
        functools.partial(shards, sizes),
        mesh=mesh,
        in_specs=placed,
        out_specs=(P(("row", "col"), None), P(("row", "col"), None)),
        check_vma=False,
    )
```

profile of v0, /device:TPU:0, one launch (start us, length us, event | category | flops | bytes accessed | tf_op | source)
XLA Modules:
  0.0 164.5 jit_solution(2187444225248317491)
XLA Ops:
  7.2 0.0 all-gather.5.cloned.1.call-start
  7.2 0.7 all-gather.5.cloned.1.call-update
  7.9 0.0 all-gather.3.cloned.1.call-start
  7.9 0.7 all-gather.3.cloned.1.call-update
  8.6 0.7 reshape.36.gain_ref
  9.3 0.7 reshape.39.gain_ref
  10.0 0.7 reshape.33.gate_ref
  10.7 1.4 copy-done.1
  12.1 0.7 copy-done.9
  12.8 0.7 copy-done.10
  13.5 2.3 %dispatch.1 = (bf16[1024,768]{1,0:T(8,128)(2,1)S(1)}, f32[32,128]{1,0:T(8,128)S(1)}) custom-call(s32[1,1024]{1,0:T(1,128)S(1)} %bitcast.10, s32[1,1024]{1,0:T(1,128)S(1)} %bitcast.11, bf16[1,1024]{1,0:T(2,128)(2,1)S(1)} %reshape.33.gate_ref, bf16[1024,768]{1,0:T(8,128)(2,1)S(1)} %copy-done.1), custom_call_target="tpu_custom_call" | custom-call | tf_op jit(solution)/shard_map/dispatch/pallas_call | solution.py:322
  15.8 1.1 copy-done.3
  16.9 0.6 copy-done.8
  17.5 43.0 %exchange1.1 = (bf16[1024,768]{1,0:T(8,128)(2,1)}, f32[32,1,128]{2,1,0:T(1,128)}) custom-call(bf16[1024,768]{1,0:T(8,128)(2,1)} %copy-done.3, f32[32,1,128]{2,1,0:T(1,128)} %bitcast.9), custom_call_target="tpu_custom_call" | custom-call | tf_op jit(solution)/shard_map/exchange1/pallas_call | solution.py:281
  60.6 1.4 copy-done
  62.0 0.7 copy-done.6
  62.7 25.4 %experts.1 = (bf16[1024,768]{1,0:T(8,128)(2,1)S(1)}, f32[32,128]{1,0:T(8,128)S(1)}) custom-call(bf16[1024,768]{1,0:T(8,128)(2,1)S(1)} %copy-done, f32[32,128]{1,0:T(8,128)S(1)} %bitcast.7, f32[1,768]{1,0:T(1,128)S(1)} %reshape.36.gain_ref, bf16[2,768,3072]{2,1,0:T(8,128)(2,1)} %in_ref.1, bf16[2,3072,768]{2,1,0:T(8,128)(2,1)} %out_ref.1), custom_call_target="tpu_custom_call" | custom-call | tf_op jit(solution)/shard_map/experts/pallas_call | solution.py:336
  88.1 1.1 copy-done.2
  89.3 0.6 copy-done.7
  89.9 40.8 %exchange2.1 = (bf16[1024,768]{1,0:T(8,128)(2,1)}, f32[32,1,128]{2,1,0:T(1,128)}) custom-call(bf16[1024,768]{1,0:T(8,128)(2,1)} %copy-done.2, f32[32,1,128]{2,1,0:T(1,128)} %bitcast.8), custom_call_target="tpu_custom_call" | custom-call | tf_op jit(solution)/shard_map/exchange2/pallas_call | solution.py:281
  130.7 0.0 all-gather.5.cloned.1.call-done
  130.7 1.6 copy.15.mix_ref
  132.4 5.9 %copy.14.qkv_ref = bf16[768,2304]{1,0:T(8,128)(2,1)} copy(bf16[768,2304]{0,1:T(8,128)(2,1)} %all-gather.3.cloned.1.call-done) | data formatting | bytes 7077888 | tf_op jit(solution)/shard_map/all_gather | solution.py:317
  138.3 19.3 %attention.1 = (bf16[1024,768]{1,0:T(8,128)(2,1)}, bf16[1024,768]{1,0:T(8,128)(2,1)}) custom-call(bf16[1024,768]{1,0:T(8,128)(2,1)S(1)} %copy-done.4, f32[32,128]{1,0:T(8,128)S(1)} %bitcast.6, f32[1,768]{1,0:T(1,128)S(1)} %reshape.39.gain_ref, bf16[768,2304]{1,0:T(8,128)(2,1)} %copy.14.qkv_ref, bf16[768,768]{1,0:T(8,128)(2,1)S(1)} %copy.15.mix_ref), custom_call_target="tpu_custom_call" | custom-call | tf_op jit(solution)/shard_map/attention/pallas_call | solution.py:360
  (14 shorter events, 0.1 us)
Async XLA Ops:
  7.2 123.6 %all-gather.5.cloned.1.call-start = ((), (), s32[]{:S(2)}) async-start(), calls=%async_computation.1 | async-start | bytes 1327104 | tf_op jit(solution)/shard_map/all_gather | solution.py:318
  7.9 124.5 %all-gather.3.cloned.1.call-start = ((), (), s32[]{:S(2)}) async-start(), calls=%async_computation | async-start | bytes 3981312 | tf_op jit(solution)/shard_map/all_gather | solution.py:317
  10.7 1.4 copy-start.1
  12.1 0.7 copy-start.9
  12.8 0.7 copy-start.10
  15.8 1.1 copy-start.3
  16.9 0.6 copy-start.8
  60.6 1.4 copy-start
  62.0 0.7 copy-start.6
  88.1 1.1 copy-start.2
  89.3 0.6 copy-start.7
  132.3 6.0 %copy-start.4 = (bf16[1024,768]{1,0:T(8,128)(2,1)S(1)}, bf16[1024,768]{1,0:T(8,128)(2,1)}, u32[]{:S(2)}) copy-start(bf16[1024,768]{1,0:T(8,128)(2,1)} %get-tuple-element.16.x_ref) | copy-start | bytes 4718596
  132.3 6.0 %copy-start.5 = (f32[32,1,128]{2,1,0:T(1,128)S(1)}, f32[32,1,128]{2,1,0:T(1,128)}, u32[]{:S(2)}) copy-start(f32[32,1,128]{2,1,0:T(1,128)} %get-tuple-element.17) | copy-start | bytes 49156
Sparse Core Ops, SparseCore 0:
  9.9 36.5 all-gather.4
  48.3 33.6 all-gather.2
where the time goes:
time: 165 us; the launch traced here: 164 us
  Pallas kernels  131 us (79%)
  local copies, waits for them, and re-layouts  17.9 us (11%)
  between operations  14.1 us (9%)
    pallas_call x2, Pallas kernels, exchange(): pl.pallas_call(functools.partial(exchange_kernel, sizes), out_shape=(jax....  83.8 us
    pallas_call x1, Pallas kernels, shards(): pl.pallas_call(functools.partial(expert_kernel, devices), out_shape=(rows...  25.4 us
    pallas_call x1, Pallas kernels, shards(): pl.pallas_call(functools.partial(attention_kernel, devices), out_shape=(r...  19.3 us
    unnamed x22, local copies, waits for them, and re-layouts  8.39 us
    all_gather x1, local copies, waits for them, and re-layouts, shards(): qkv_full = lax.all_gather(qkv_weight, 'row', axis=1, tiled=True)  5.91 us
  transfers between devices with their start and end apart: 2, of which 0 were waited for; matrix products, arithmetic and copies ran while one was open for 2% of the time, Pallas kernels for 68%

commit v1 on v0

--- a/solution.py
+++ b/solution.py
@@ -99,7 +99,7 @@
 
 
 def expert_kernel(
-    devices, x_ref, meta_ref, gain_ref, in_ref, out_ref, y_ref, meta2_ref, xs, inputs, total, info, places
+    devices, x_ref, meta_ref, gain_ref, in_ref, out_ref, y_ref, meta2_ref, xs, inputs, total, info, places, split
 ):
     rows, width = x_ref.shape
     per = rows // devices
@@ -146,10 +146,20 @@
                 low_row = i * step - (rows - cap)
                 inputs[1, low_row : low_row + step] = jnp.where(is_first, none, normed)
         total[...] = jnp.zeros_like(total)
-
-    base = pl.multiple_of(expert * (rows - cap), rows - cap)
-    hidden = jnp.maximum(dot(inputs[expert], in_ref[0]), 0.0).astype(BF16)
-    total[pl.ds(base, cap), :] += dot(hidden, out_ref[0])
+        split[0] = jnp.sum(jnp.where(local == 0, 1.0, 0.0)).astype(I32)
+
+    tile = rows // 4
+    own_rows = jnp.where(expert == 0, split[0], rows - split[0])
+    for tiles in range(1, cap // tile + 1):
+        size = tiles * tile
+
+        @pl.when((own_rows <= size) & (own_rows > size - tile))
+        def _():
+            source = pl.multiple_of(expert * (cap - size), tile)
+            base = pl.multiple_of(expert * (rows - size), tile)
+            wide = dot(inputs[expert, pl.ds(source, size)], in_ref[0])
+            hidden = jnp.maximum(wide, 0.0).astype(BF16)
+            total[pl.ds(base, size), :] += dot(hidden, out_ref[0])
 
     @pl.when((expert == 1) & (chunk == pl.num_programs(1) - 1))
     def _():
@@ -174,7 +184,7 @@
     normed = rms_scale(moved, gain_ref[...])
     for i in range(3):
         part = slice(i * width, (i + 1) * width)
-        qkv[:, part] = dot(normed, qkv_ref[:, part]).astype(BF16)
+        qkv[:, part] = dot_nt(normed, qkv_ref[part]).astype(BF16)
     scale = 1.0 / HEAD_DIM**0.5
     left = iota((seq, LANES), 1) < HEAD_DIM
     ones = jnp.ones((seq, LANES), BF16)
@@ -191,14 +201,14 @@
             mixed = dot(weights, values)
             halves.append(mixed[:, :LANES] / mixed[:, LANES:])
         context[:, at : at + LANES] = jnp.where(left, halves[0], halves[1]).astype(BF16)
-    branch_ref[...] = dot(context[...], mix_ref[...]).astype(BF16)
-
-
-def exchange_kernel(sizes, x_ref, m_ref, y_ref, n_ref, send, recv, send_meta, recv_meta, own):
+    branch_ref[...] = dot_nt(context[...], mix_ref[...]).astype(BF16)
+
+
+def peers(sizes):
     n_row, n_col = sizes
     devices = n_row * n_col
-    per = x_ref.shape[0] // devices
-    me = lax.axis_index("row") * n_col + lax.axis_index("col")
+    row, col = lax.axis_index("row"), lax.axis_index("col")
+    me = row * n_col + col
 
     def peer_of(i):
         return lax.rem(me + i, devices)
@@ -206,9 +216,11 @@
     def coords(device):
         return (device // n_col, lax.rem(device, n_col))
 
-    def block(ref, device):
-        return ref.at[pl.ds(pl.multiple_of(device * per, per), per)]
-
+    return row, col, me, peer_of, coords
+
+
+def greet_all(sizes):
+    _, _, _, peer_of, coords = peers(sizes)
     barrier = pltpu.get_barrier_semaphore()
 
     def greet(i, carry):
@@ -217,80 +229,212 @@
         )
         return carry
 
-    lax.fori_loop(1, devices, greet, 0)
-    mine = [
-        pltpu.make_async_copy(block(x_ref, me), block(y_ref, me), own.at[0]),
-        pltpu.make_async_copy(m_ref.at[me], n_ref.at[me], own.at[1]),
+    lax.fori_loop(1, sizes[0] * sizes[1], greet, 0)
+    return barrier
+
+
+def remote(source, landing, send, recv, device):
+    return pltpu.make_async_remote_copy(
+        src_ref=source,
+        dst_ref=landing,
+        send_sem=send,
+        recv_sem=recv,
+        device_id=device,
+        device_id_type=pl.DeviceIdType.MESH,
+    )
+
+
+def rows_exchange(sizes, x_ref, m_ref, y_ref, n_ref, send, recv, send_meta, recv_meta, own):
+    devices = sizes[0] * sizes[1]
+    per = x_ref.shape[0] // devices
+    _, _, me, peer_of, coords = peers(sizes)
+
+    def block(ref, device):
+        return ref.at[pl.ds(pl.multiple_of(device * per, per), per)]
+
+    def mine():
+        return (
+            pltpu.make_async_copy(block(x_ref, me), block(y_ref, me), own.at[0]),
+            pltpu.make_async_copy(m_ref.at[me], n_ref.at[me], own.at[1]),
+        )
+
+    def copies(i, landing):
+        peer = peer_of(i)
+        target = coords(peer)
+        return (
+            remote(m_ref.at[peer], n_ref.at[landing], send_meta.at[i], recv_meta.at[i], target),
+            remote(block(x_ref, peer), block(y_ref, landing), send.at[i], recv.at[i], target),
+        )
+
+    def start():
+        def begin(i, carry):
+            for copy in copies(i, me):
+                copy.start()
+            return carry
+
+        for copy in mine():
+            copy.start()
+        lax.fori_loop(1, devices, begin, 0)
+
+    def end():
+        def finish(i, carry):
+            for copy in copies(i, lax.rem(me + devices - i, devices)):
+                copy.wait_send()
+                copy.wait_recv()
+            return carry
+
+        for copy in mine():
+            copy.wait()
+        lax.fori_loop(1, devices, finish, 0)
+
+    return start, end
+
+
+def exchange1_kernel(sizes, x_ref, m_ref, w_ref, y_ref, n_ref, held_ref, *sems):
+    chips = sizes[0] // 2
+    row, col, _, _, _ = peers(sizes)
+    chip, core = row // 2, lax.rem(row, 2)
+    send_w, recv_w = sems[5:]
+    start, end = rows_exchange(sizes, x_ref, m_ref, y_ref, n_ref, *sems[:5])
+    barrier = greet_all(sizes)
+    own = pltpu.make_async_copy(w_ref, held_ref.at[chip], send_w.at[0])
+    own.start()
+    pl.semaphore_wait(barrier, sizes[0] * sizes[1] - 1)
+    start()
+
+    def weights(i, landing):
+        target = (lax.rem(chip + i, chips) * 2 + core, col)
+        return remote(w_ref, held_ref.at[landing], send_w.at[i], recv_w.at[i], target)
+
+    for i in range(1, chips):
+        weights(i, chip).start()
+    own.wait()
+    for i in range(1, chips):
+        weights(i, lax.rem(chip + chips - i, chips)).wait()
+    end()
+
+
+def exchange2_kernel(
+    sizes, x_ref, m_ref, held_ref, mix_ref, y_ref, n_ref, wide_ref, full_ref, *sems
+):
+    n_row = sizes[0]
+    chips, columns, _ = held_ref.shape
+    mix_columns = mix_ref.shape[0]
+    row, col, _, _, _ = peers(sizes)
+    core = lax.rem(row, 2)
+    local_w, send_w, recv_w, send_x, recv_x = sems[5:]
+    start, end = rows_exchange(sizes, x_ref, m_ref, y_ref, n_ref, *sems[:5])
+    barrier = greet_all(sizes)
+
+    def part(ref, index, size):
+        return ref.at[pl.ds(pl.multiple_of(index * size, size), size)]
+
+    owned = [
+        pltpu.make_async_copy(held_ref.at[c], part(wide_ref, 2 * c + core, columns), local_w.at[c])
+        for c in range(chips)
     ]
-    for copy in mine:
+    owned.append(pltpu.make_async_copy(mix_ref, part(full_ref, row, mix_columns), local_w.at[chips]))
+    for copy in owned:
         copy.start()
-    pl.semaphore_wait(barrier, devices - 1)
-
-    def copies(i, target, landing):
-        peer = peer_of(i)
-        return (
-            pltpu.make_async_remote_copy(
-                src_ref=m_ref.at[peer],
-                dst_ref=n_ref.at[landing],
-                send_sem=send_meta.at[i],
-                recv_sem=recv_meta.at[i],
-                device_id=coords(target),
-                device_id_type=pl.DeviceIdType.MESH,
-            ),
-            pltpu.make_async_remote_copy(
-                src_ref=block(x_ref, peer),
-                dst_ref=block(y_ref, landing),
-                send_sem=send.at[i],
-                recv_sem=recv.at[i],
-                device_id=coords(target),
-                device_id_type=pl.DeviceIdType.MESH,
-            ),
-        )
-
-    def begin(i, carry):
-        for copy in copies(i, peer_of(i), me):
-            copy.start()
-        return carry
-
-    lax.fori_loop(1, devices, begin, 0)
-
-    def finish(i, carry):
-        source = lax.rem(me + devices - i, devices)
-        for copy in copies(i, peer_of(i), source):
-            copy.wait_send()
-            copy.wait_recv()
-        return carry
-
-    lax.fori_loop(1, devices, finish, 0)
-    for copy in mine:
+    pl.semaphore_wait(barrier, sizes[0] * sizes[1] - 1)
+    sibling = (row + 1 - 2 * core, col)
+
+    def weights(c, side):
+        landing = part(wide_ref, 2 * c + side, columns)
+        return remote(held_ref.at[c], landing, send_w.at[c], recv_w.at[c], sibling)
+
+    def mixing(i, landing):
+        target = (lax.rem(row + i, n_row), col)
+        landing = part(full_ref, landing, mix_columns)
+        return remote(mix_ref, landing, send_x.at[i], recv_x.at[i], target)
+
+    start()
+    for c in range(chips):
+        weights(c, core).start()
+    for i in range(1, n_row):
+        mixing(i, row).start()
+    for copy in owned:
         copy.wait()
-
-
-def exchange(x, meta, sizes, collective_id):
+    for c in range(chips):
+        weights(c, 1 - core).wait()
+    for i in range(1, n_row):
+        mixing(i, lax.rem(row + n_row - i, n_row)).wait()
+    end()
+
+
+def exchange_first(sizes, x, meta, qkv_weight, mix_weight):
     devices = sizes[0] * sizes[1]
     rows, width = x.shape
-    per = rows // devices
     meta = meta.reshape(devices, 1, LANES)
-    if per % 16:
-        y = lax.all_to_all(
-            x.reshape(devices, per, width), ("row", "col"), split_axis=0, concat_axis=0, tiled=True
+    if rows // devices % 16 or sizes[0] % 2:
+        held = (
+            lax.all_gather(qkv_weight, "row", axis=0, tiled=True),
+            lax.all_gather(mix_weight, "row", axis=0, tiled=True),
         )
-        n = lax.all_to_all(meta, ("row", "col"), split_axis=0, concat_axis=0, tiled=True)
-        return y.reshape(rows, width), n.reshape(devices, LANES)
-    anywhere = pl.BlockSpec(memory_space=pl.ANY)
-    y, n = pl.pallas_call(
-        functools.partial(exchange_kernel, sizes),
+        return *all_to_all(devices, x, meta), held
+    vmem = pl.BlockSpec()
+    hbm = pl.BlockSpec(memory_space=pl.ANY)
+    chips = sizes[0] // 2
+    y, n, held = pl.pallas_call(
+        functools.partial(exchange1_kernel, sizes),
         out_shape=(
             jax.ShapeDtypeStruct(x.shape, x.dtype),
             jax.ShapeDtypeStruct(meta.shape, meta.dtype),
+            jax.ShapeDtypeStruct((chips, *qkv_weight.shape), BF16),
         ),
-        in_specs=[anywhere] * 2,
-        out_specs=(anywhere, anywhere),
-        scratch_shapes=[pltpu.SemaphoreType.DMA((devices,))] * 4 + [pltpu.SemaphoreType.DMA((2,))],
-        compiler_params=pltpu.CompilerParams(collective_id=collective_id, has_side_effects=True),
-        name="exchange%d" % collective_id,
-    )(x, meta)
-    return y, n.reshape(devices, LANES)
+        in_specs=[vmem, vmem, hbm],
+        out_specs=(vmem, vmem, hbm),
+        scratch_shapes=[pltpu.SemaphoreType.DMA((devices,))] * 4
+        + [pltpu.SemaphoreType.DMA((2,))]
+        + [pltpu.SemaphoreType.DMA((chips,))] * 2,
+        compiler_params=pltpu.CompilerParams(
+            collective_id=1, has_side_effects=True, vmem_limit_bytes=32 * MIB
+        ),
+        name="exchange1",
+    )(x, meta, qkv_weight)
+    return y, n.reshape(devices, LANES), held
+
+
+def all_to_all(devices, x, meta):
+    rows, width = x.shape
+    y, n = (
+        lax.all_to_all(part, ("row", "col"), split_axis=0, concat_axis=0, tiled=True)
+        for part in (x.reshape(devices, rows // devices, width), meta)
+    )
+    return y.reshape(rows, width), n.reshape(devices, LANES)
+
+
+def exchange_second(sizes, x, meta, held, mix_weight):
+    devices = sizes[0] * sizes[1]
+    rows, width = x.shape
+    meta = meta.reshape(devices, 1, LANES)
+    if rows // devices % 16 or sizes[0] % 2:
+        return *all_to_all(devices, x, meta), *held
+    vmem = pl.BlockSpec()
+    hbm = pl.BlockSpec(memory_space=pl.ANY)
+    n_row = sizes[0]
+    chips, columns, depth = held.shape
+    y, n, wide, full = pl.pallas_call(
+        functools.partial(exchange2_kernel, sizes),
+        out_shape=(
+            jax.ShapeDtypeStruct(x.shape, x.dtype),
+            jax.ShapeDtypeStruct(meta.shape, meta.dtype),
+            jax.ShapeDtypeStruct((n_row * columns, depth), BF16),
+            jax.ShapeDtypeStruct((n_row * mix_weight.shape[0], depth), BF16),
+        ),
+        in_specs=[vmem, vmem, hbm, hbm],
+        out_specs=(vmem,) * 4,
+        scratch_shapes=[pltpu.SemaphoreType.DMA((devices,))] * 4
+        + [pltpu.SemaphoreType.DMA((2,))]
+        + [pltpu.SemaphoreType.DMA((chips + 1,))]
+        + [pltpu.SemaphoreType.DMA((chips,))] * 2
+        + [pltpu.SemaphoreType.DMA((n_row,))] * 2,
+        compiler_params=pltpu.CompilerParams(
+            collective_id=2, has_side_effects=True, vmem_limit_bytes=40 * MIB
+        ),
+        name="exchange2",
+    )(x, meta, held, mix_weight)
+    return y, n.reshape(devices, LANES), wide, full
 
 
 def whole(shape):
@@ -314,9 +458,8 @@
     devices = sizes[0] * sizes[1]
     hidden = expert_in.shape[2]
     cap = rows * 3 // 4
-    qkv_full = lax.all_gather(qkv_weight, "row", axis=1, tiled=True)
-    mix_full = lax.all_gather(mix_weight, "row", axis=1, tiled=True)
     meta_shape = jax.ShapeDtypeStruct((devices, LANES), F32)
+    qkv_weight, mix_weight = qkv_weight.T, mix_weight.T
     rows_shape = jax.ShapeDtypeStruct((rows, width), BF16)
 
     leaving, meta = pl.pallas_call(
@@ -330,7 +473,7 @@
         gate_prob.reshape(1, rows),
         tokens,
     )
-    arrived, meta = exchange(leaving, meta, sizes, 1)
+    arrived, meta, held = exchange_first(sizes, leaving, meta, qkv_weight, mix_weight)
 
     chunk = hidden // 4
     leaving, meta = pl.pallas_call(
@@ -351,11 +494,12 @@
             pltpu.VMEM((rows, width), F32),
             pltpu.VMEM((rows, LANES), F32),
             pltpu.VMEM((8, rows), F32),
+            pltpu.SMEM((1,), I32),
         ],
         compiler_params=pltpu.CompilerParams(vmem_limit_bytes=48 * MIB),
         name="experts",
     )(arrived, meta, ff_gain.reshape(1, width), expert_in, expert_out)
-    arrived, meta = exchange(leaving, meta, sizes, 2)
+    arrived, meta, qkv_full, mix_full = exchange_second(sizes, leaving, meta, held, mix_weight)
 
     return pl.pallas_call(
         functools.partial(attention_kernel, devices),
@@ -365,7 +509,7 @@
             whole((rows, width)),
             whole((devices, LANES)),
             whole((1, width)),
-            whole((width, 3 * width)),
+            whole((3 * width, width)),
             whole((width, width)),
         ],
         out_specs=(
@@ -376,7 +520,7 @@
             pltpu.VMEM((SEQ, 3 * width), BF16),
             pltpu.VMEM((SEQ, width), BF16),
         ],
-        compiler_params=pltpu.CompilerParams(vmem_limit_bytes=48 * MIB),
+        compiler_params=pltpu.CompilerParams(vmem_limit_bytes=32 * MIB),
         name="attention",
     )(arrived, meta, attn_gain.reshape(1, width), qkv_full, mix_full)
 

time: 165 us -> 135 us (0.82)
  local copies, waits for them, and re-layouts: 17.9 us -> 3.5 us
  between operations: 14.1 us -> 0.73 us
    all_gather x2 -> x0, local copies, waits for them, and re-layouts: 7.48 us -> none  [the longest x1 5.91 us: shards(): qkv_full = lax.all_gather(qkv_weight, 'row', axis=1, tiled=True)]
    unnamed x22 -> x14, local copies, waits for them, and re-layouts: 8.39 us -> 2.8 us
    pallas_call x2, Pallas kernels: 83.8 us -> 87.9 us  [the longest x1 47.8 us: exchange_first(): pl.pallas_call(functools.partial(exchange1_kernel, sizes), out_shape=(jax...]
    pallas_call x1, Pallas kernels: 25.4 us -> 23.3 us  [shards(): pl.pallas_call(functools.partial(expert_kernel, devices), out_shape=(rows...]
    pallas_call x1, Pallas kernels: 19.3 us -> 17.3 us  [shards(): pl.pallas_call(functools.partial(attention_kernel, devices), out_shape=(r...]
  transfers between devices with their start and end apart: 2 -> 0, of which waited for: 0 -> 0; matrix products, arithmetic and copies ran while one was open for 2% -> 0% of each run, Pallas kernels for 68% -> 0%
where the time goes in v1:
time: 135 us
  Pallas kernels  131 us (97%)
  local copies, waits for them, and re-layouts  3.5 us (3%)
    pallas_call x1, Pallas kernels, exchange_first(): pl.pallas_call(functools.partial(exchange1_kernel, sizes), out_shape=(jax...  47.8 us
    pallas_call x1, Pallas kernels, exchange_second(): pl.pallas_call(functools.partial(exchange2_kernel, sizes), out_shape=(jax...  40.1 us
    pallas_call x1, Pallas kernels, shards(): pl.pallas_call(functools.partial(expert_kernel, devices), out_shape=(rows...  23.3 us
    pallas_call x1, Pallas kernels, shards(): pl.pallas_call(functools.partial(attention_kernel, devices), out_shape=(r...  17.3 us
    unnamed x14, local copies, waits for them, and re-layouts  2.8 us

profile of v1, /device:TPU:0, one launch (start us, length us, event | category | flops | bytes accessed | tf_op | source)
XLA Modules:
  0.0 135.0 jit_solution(13028061634017858374)
XLA Ops:
  0.6 0.7 reshape.33.gate_ref
  1.3 0.0 copy-start
  1.3 1.4 %copy-done = bf16[1024,768]{1,0:T(8,128)(2,1)S(1)} copy-done((bf16[1024,768]{1,0:T(8,128)(2,1)S(1)}, bf16[1024,768]{1,0:T(8,128)(2,1)}, u32[]{:S(2)}) %copy-start) | copy-done | bytes 1572888
  2.7 0.0 copy-start.3
  2.7 0.7 copy-done.3
  3.4 0.0 copy-start.4
  3.4 0.7 copy-done.4
  4.1 0.0 copy-start.1
  4.1 0.0 copy-start.5
  4.1 2.3 %dispatch.1 = (bf16[1024,768]{1,0:T(8,128)(2,1)S(1)}, f32[32,128]{1,0:T(8,128)S(1)}) custom-call(s32[1,1024]{1,0:T(1,128)S(1)} %bitcast.14, s32[1,1024]{1,0:T(1,128)S(1)} %bitcast.15, bf16[1,1024]{1,0:T(2,128)(2,1)S(1)} %reshape.33.gate_ref, bf16[1024,768]{1,0:T(8,128)(2,1)S(1)} %copy-done), custom_call_target="tpu_custom_call" | custom-call | tf_op jit(solution)/shard_map/dispatch/pallas_call | solution.py:465
  6.4 0.0 copy-done.1
  6.4 47.8 %exchange1.1 = (bf16[1024,768]{1,0:T(8,128)(2,1)S(1)}, f32[32,1,128]{2,1,0:T(1,128)S(1)}, bf16[4,288,768]{2,1,0:T(8,128)(2,1)S(1)}) custom-call(bf16[1024,768]{1,0:T(8,128)(2,1)S(1)} %get-tuple-element.13.x_ref, f32[32,1,128]{2,1,0:T(1,128)S(1)} %bitcast.13, bf16[288,768]{1,0:T(8,128)(2,1)S(1)} %bitcast.8), custom_call_target="tpu_custom_call" | custom-call | tf_op jit(solution)/shard_map/exchange1/pallas_call | solution.py:378
  54.2 0.0 copy-done.5
  54.2 0.0 copy-start.2
  54.2 23.3 %experts.1 = (bf16[1024,768]{1,0:T(8,128)(2,1)S(1)}, f32[32,128]{1,0:T(8,128)S(1)}) custom-call(bf16[1024,768]{1,0:T(8,128)(2,1)S(1)} %get-tuple-element.15.x_ref, f32[32,128]{1,0:T(8,128)S(1)} %bitcast.12, f32[1,768]{1,0:T(1,128)S(1)} %reshape.36.gain_ref, bf16[2,768,3072]{2,1,0:T(8,128)(2,1)} %in_ref.1, bf16[2,3072,768]{2,1,0:T(8,128)(2,1)} %out_ref.1), custom_call_target="tpu_custom_call" | custom-call | tf_op jit(solution)/shard_map/experts/pallas_call | solution.py:479
  77.6 0.0 copy-done.2
  77.6 0.0 copy-start.6
  77.6 40.1 %exchange2.1 = (bf16[1024,768]{1,0:T(8,128)(2,1)S(1)}, f32[32,1,128]{2,1,0:T(1,128)S(1)}, bf16[2304,768]{1,0:T(8,128)(2,1)S(1)}, bf16[768,768]{1,0:T(8,128)(2,1)S(1)}) custom-call(bf16[1024,768]{1,0:T(8,128)(2,1)S(1)} %get-tuple-element.17.x_ref, f32[32,1,128]{2,1,0:T(1,128)S(1)} %bitcast.10, bf16[4,288,768]{2,1,0:T(8,128)(2,1)S(1)} %get-tuple-element.19.held_ref, ...), custom_call_target="tpu_custom_call" | custom-call | tf_op jit(solution)/shard_map/exchange2/pallas_call | solution.py:417
  117.7 0.0 copy-done.6
  117.7 17.3 %attention.1 = (bf16[1024,768]{1,0:T(8,128)(2,1)}, bf16[1024,768]{1,0:T(8,128)(2,1)}) custom-call(bf16[1024,768]{1,0:T(8,128)(2,1)S(1)} %get-tuple-element.20.x_ref, f32[32,128]{1,0:T(8,128)S(1)} %bitcast.11, f32[1,768]{1,0:T(1,128)S(1)} %reshape.39.gain_ref, bf16[2304,768]{1,0:T(8,128)(2,1)S(1)} %get-tuple-element.22.qkv_ref, ...), custom_call_target="tpu_custom_call" | custom-call | tf_op jit(solution)/shard_map/attention/pallas_call | solution.py:504
  (2 shorter events, 0.0 us)
Async XLA Ops:
  1.3 1.4 %copy-start = (bf16[1024,768]{1,0:T(8,128)(2,1)S(1)}, bf16[1024,768]{1,0:T(8,128)(2,1)}, u32[]{:S(2)}) copy-start(bf16[1024,768]{1,0:T(8,128)(2,1)} %tok_ref.1) | copy-start | bytes 4718596
  2.7 0.7 copy-start.3
  3.4 0.7 copy-start.4
  4.1 2.3 %copy-start.1 = (bf16[768,288]{0,1:T(8,128)(2,1)S(1)}, bf16[768,288]{0,1:T(8,128)(2,1)}, u32[]{:S(2)}) copy-start(bf16[768,288]{0,1:T(8,128)(2,1)} %param.18) | copy-start | bytes 1327108
  4.1 50.1 %copy-start.5 = (f32[768]{0:T(1024)S(1)}, f32[768]{0:T(1024)}, u32[]{:S(2)}) copy-start(f32[768]{0:T(1024)} %param.14) | copy-start | bytes 9220
  54.2 23.4 %copy-start.2 = (bf16[768,96]{0,1:T(8,128)(2,1)S(1)}, bf16[768,96]{0,1:T(8,128)(2,1)}, u32[]{:S(2)}) copy-start(bf16[768,96]{0,1:T(8,128)(2,1)} %param.19) | copy-start | bytes 442372
  77.6 40.1 %copy-start.6 = (f32[768]{0:T(1024)S(1)}, f32[768]{0:T(1024)}, u32[]{:S(2)}) copy-start(f32[768]{0:T(1024)} %param.17) | copy-start | bytes 9220

commit v2 on v1

--- a/solution.py
+++ b/solution.py
@@ -72,9 +72,16 @@
     return dot_nt(pick, spreaded)
 
 
-def dispatch_kernel(devices, id_ref, dest_ref, gate_ref, tok_ref, out_ref, meta_ref):
+def dispatch_kernel(devices, id_hbm, dest_hbm, gate_ref, tok_hbm, out_ref, meta_ref, *scratch):
+    id_ref, dest_ref, tok_ref, sems = scratch
     rows = tok_ref.shape[0]
     per = rows // devices
+    pairs = ((id_hbm, id_ref), (dest_hbm, dest_ref), (tok_hbm, tok_ref))
+    copies = [pltpu.make_async_copy(*pair, sems.at[i]) for i, pair in enumerate(pairs)]
+    for copy in copies:
+        copy.start()
+    copies[0].wait()
+    copies[1].wait()
     ids = id_ref[...]
     dest = dest_ref[...]
     target = ids // 2
@@ -93,6 +100,7 @@
     meta_ref[...] = to_blocks(onehot, rank, fields, per)
     position = target * per + rank
     step = rows // 4
+    copies[2].wait()
     for i in range(4):
         part = permute(position, rows, tok_ref[...], i * step, step)
         out_ref[i * step : (i + 1) * step, :] = part.astype(BF16)
@@ -116,13 +124,14 @@
         local = code // DIGIT
         low = code - local * DIGIT
         onehot = one(iota((devices, rows), 0) == owner)
-        first = one(jnp.broadcast_to(local == 0, (8, rows)))
-        upper = earlier(rows)
-        counts = dot(onehot, upper)
-        rank2 = jnp.sum(onehot.astype(F32) * counts, axis=0, keepdims=True).astype(I32)
+        is_local = jnp.where(local == 0, 1.0, 0.0)
+        first = jnp.broadcast_to(is_local, (16, rows)).astype(BF16)
+        counts = dot(jnp.concatenate([onehot, first], axis=0), earlier(rows))
+        ranked = onehot.astype(F32) * counts[:devices]
+        rank2 = jnp.sum(ranked, axis=0, keepdims=True).astype(I32)
         meta2_ref[...] = to_blocks(onehot, rank2, [low.astype(F32), high.astype(F32)], per)
         leave = owner * per + rank2
-        before = dot(first, upper)[0:1].astype(I32)
+        before = counts[devices : devices + 1].astype(I32)
         number = jnp.sum(jnp.where(local == 0, 1.0, 0.0), axis=1, keepdims=True).astype(I32)
         position = jnp.where(local == 0, before, number + iota((1, rows), 1) - before)
         sort = one(iota((rows, rows), 0) == position)
@@ -465,6 +474,18 @@
     leaving, meta = pl.pallas_call(
         functools.partial(dispatch_kernel, devices),
         out_shape=(rows_shape, meta_shape),
+        in_specs=[
+            pl.BlockSpec(memory_space=pl.ANY),
+            pl.BlockSpec(memory_space=pl.ANY),
+            pl.BlockSpec(),
+            pl.BlockSpec(memory_space=pl.ANY),
+        ],
+        scratch_shapes=[
+            pltpu.VMEM((1, rows), I32),
+            pltpu.VMEM((1, rows), I32),
+            pltpu.VMEM((rows, width), BF16),
+            pltpu.SemaphoreType.DMA((3,)),
+        ],
         compiler_params=pltpu.CompilerParams(vmem_limit_bytes=32 * MIB),
         name="dispatch",
     )(

time: 135 us -> 135 us (level)
  no operation moved by 1% of the time
where the time goes in v2:
time: 135 us
  Pallas kernels  131 us (97%)
  local copies, waits for them, and re-layouts  3.5 us (3%)
    pallas_call x1, Pallas kernels, exchange_first(): pl.pallas_call(functools.partial(exchange1_kernel, sizes), out_shape=(jax...  47.8 us
    pallas_call x1, Pallas kernels, exchange_second(): pl.pallas_call(functools.partial(exchange2_kernel, sizes), out_shape=(jax...  41 us
    pallas_call x1, Pallas kernels, shards(): pl.pallas_call(functools.partial(expert_kernel, devices), out_shape=(rows...  22.1 us
    pallas_call x1, Pallas kernels, shards(): pl.pallas_call(functools.partial(attention_kernel, devices), out_shape=(r...  17.1 us
    unnamed x14, local copies, waits for them, and re-layouts  2.8 us

profile of v2, /device:TPU:0, one launch (start us, length us, event | category | flops | bytes accessed | tf_op | source)
XLA Modules:
  0.0 134.8 jit_solution(16730829862994299180)
XLA Ops:
  0.6 0.7 reshape.33.gate_ref
  1.3 0.0 copy-start
  1.3 1.4 %copy-done = bf16[1024,768]{1,0:T(8,128)(2,1)S(1)} copy-done((bf16[1024,768]{1,0:T(8,128)(2,1)S(1)}, bf16[1024,768]{1,0:T(8,128)(2,1)}, u32[]{:S(2)}) %copy-start) | copy-done | bytes 1572888
  2.7 0.0 copy-start.3
  2.7 0.7 copy-done.3
  3.4 0.0 copy-start.4
  3.4 0.7 copy-done.4
  4.1 0.0 copy-start.1
  4.1 0.0 copy-start.5
  4.1 2.6 %dispatch.1 = (bf16[1024,768]{1,0:T(8,128)(2,1)S(1)}, f32[32,128]{1,0:T(8,128)S(1)}) custom-call(s32[1,1024]{1,0:T(1,128)S(1)} %bitcast.14, s32[1,1024]{1,0:T(1,128)S(1)} %bitcast.15, bf16[1,1024]{1,0:T(2,128)(2,1)S(1)} %reshape.33.gate_ref, bf16[1024,768]{1,0:T(8,128)(2,1)S(1)} %copy-done), custom_call_target="tpu_custom_call" | custom-call | tf_op jit(solution)/shard_map/dispatch/pallas_call | solution.py:474
  6.7 0.0 copy-done.1
  6.7 47.8 %exchange1.1 = (bf16[1024,768]{1,0:T(8,128)(2,1)S(1)}, f32[32,1,128]{2,1,0:T(1,128)S(1)}, bf16[4,288,768]{2,1,0:T(8,128)(2,1)S(1)}) custom-call(bf16[1024,768]{1,0:T(8,128)(2,1)S(1)} %get-tuple-element.13.x_ref, f32[32,1,128]{2,1,0:T(1,128)S(1)} %bitcast.13, bf16[288,768]{1,0:T(8,128)(2,1)S(1)} %bitcast.8), custom_call_target="tpu_custom_call" | custom-call | tf_op jit(solution)/shard_map/exchange1/pallas_call | solution.py:387
  54.5 0.0 copy-done.5
  54.5 0.0 copy-start.2
  54.5 22.1 %experts.1 = (bf16[1024,768]{1,0:T(8,128)(2,1)S(1)}, f32[32,128]{1,0:T(8,128)S(1)}) custom-call(bf16[1024,768]{1,0:T(8,128)(2,1)S(1)} %get-tuple-element.15.x_ref, f32[32,128]{1,0:T(8,128)S(1)} %bitcast.12, f32[1,768]{1,0:T(1,128)S(1)} %reshape.36.gain_ref, bf16[2,768,3072]{2,1,0:T(8,128)(2,1)} %in_ref.1, bf16[2,3072,768]{2,1,0:T(8,128)(2,1)} %out_ref.1), custom_call_target="tpu_custom_call" | custom-call | tf_op jit(solution)/shard_map/experts/pallas_call | solution.py:500
  76.6 0.0 copy-done.2
  76.6 0.0 copy-start.6
  76.7 41.0 %exchange2.1 = (bf16[1024,768]{1,0:T(8,128)(2,1)S(1)}, f32[32,1,128]{2,1,0:T(1,128)S(1)}, bf16[2304,768]{1,0:T(8,128)(2,1)S(1)}, bf16[768,768]{1,0:T(8,128)(2,1)S(1)}) custom-call(bf16[1024,768]{1,0:T(8,128)(2,1)S(1)} %get-tuple-element.17.x_ref, f32[32,1,128]{2,1,0:T(1,128)S(1)} %bitcast.10, bf16[4,288,768]{2,1,0:T(8,128)(2,1)S(1)} %get-tuple-element.19.held_ref, ...), custom_call_target="tpu_custom_call" | custom-call | tf_op jit(solution)/shard_map/exchange2/pallas_call | solution.py:426
  117.7 0.0 copy-done.6
  117.7 17.1 %attention.1 = (bf16[1024,768]{1,0:T(8,128)(2,1)}, bf16[1024,768]{1,0:T(8,128)(2,1)}) custom-call(bf16[1024,768]{1,0:T(8,128)(2,1)S(1)} %get-tuple-element.20.x_ref, f32[32,128]{1,0:T(8,128)S(1)} %bitcast.11, f32[1,768]{1,0:T(1,128)S(1)} %reshape.39.gain_ref, bf16[2304,768]{1,0:T(8,128)(2,1)S(1)} %get-tuple-element.22.qkv_ref, ...), custom_call_target="tpu_custom_call" | custom-call | tf_op jit(solution)/shard_map/attention/pallas_call | solution.py:525
  (2 shorter events, 0.0 us)
Async XLA Ops:
  1.3 1.4 %copy-start = (bf16[1024,768]{1,0:T(8,128)(2,1)S(1)}, bf16[1024,768]{1,0:T(8,128)(2,1)}, u32[]{:S(2)}) copy-start(bf16[1024,768]{1,0:T(8,128)(2,1)} %tok_hbm.1) | copy-start | bytes 4718596
  2.7 0.7 copy-start.3
  3.4 0.7 copy-start.4
  4.1 2.6 %copy-start.1 = (bf16[768,288]{0,1:T(8,128)(2,1)S(1)}, bf16[768,288]{0,1:T(8,128)(2,1)}, u32[]{:S(2)}) copy-start(bf16[768,288]{0,1:T(8,128)(2,1)} %param.18) | copy-start | bytes 1327108
  4.1 50.4 %copy-start.5 = (f32[768]{0:T(1024)S(1)}, f32[768]{0:T(1024)}, u32[]{:S(2)}) copy-start(f32[768]{0:T(1024)} %param.14) | copy-start | bytes 9220
  54.5 22.1 %copy-start.2 = (bf16[768,96]{0,1:T(8,128)(2,1)S(1)}, bf16[768,96]{0,1:T(8,128)(2,1)}, u32[]{:S(2)}) copy-start(bf16[768,96]{0,1:T(8,128)(2,1)} %param.19) | copy-start | bytes 442372
  76.6 41.1 %copy-start.6 = (f32[768]{0:T(1024)S(1)}, f32[768]{0:T(1024)}, u32[]{:S(2)}) copy-start(f32[768]{0:T(1024)} %param.17) | copy-start | bytes 9220
